TPU v7x, 512 devices: a whole 4x8x8 slice. The times are simulated.
512 devices in a mesh: adapter: 32 (over x, z), tensor: 16 (over y, core).
Axes of the slice: x: 4, y: 8, z: 8, core: 2. Of those that a mesh axis runs over, the one named last changes fastest.
Arguments:
- tokens: bfloat16 [32768, 8192], P('adapter', 'tensor'), may hold values from -6 to 6
- row_adapter_index: int32 [32768, 1], P('adapter'), may hold values from 0 to 511; in each aligned block of 1024 rows (0 to 1023, 1024 to 2047, ...) at most 4 rows name the same one
- adapter_down_weight: bfloat16 [512, 8192, 64], P('adapter', 'tensor'), may hold values from -0.0625 to 0.0625
- adapter_up_weight: bfloat16 [512, 64, 2048], P('adapter', None, 'tensor'), may hold values from -0.75 to 0.75
- key_value_weight: bfloat16 [8192, 2048], P('tensor'), may hold values from -0.09375 to 0.09375
- accepted_branch_rows: int32 [32, 32, 4], P('adapter'), may hold values from 0 to 1023, as said below
- owner_cache_slots: int32 [32, 32, 4], P(None, 'adapter'), may hold values from 0 to 127, as said below
Outputs:
- key_value: bfloat16 [32768, 2048], P('adapter', 'tensor')
- decode_cache: bfloat16 [4096, 2048], P('adapter', 'tensor')
Inputs may be any that keep to these rules, and one draw needn't show every extreme that they name: `row_adapter_index`: among the rows of one device no adapter is named by more than 4 rows; in the rows of some device some adapter is named by exactly 4. For each s the 128 entries accepted_branch_rows[s] are distinct. For each owner o the entries owner_cache_slots[:, o, :] name every slot of 0 to 127 once.
All inputs are finite; a program needn't handle non-finite values.
Results may differ from a plain program's by a relative error of at most 0.025.
Values may be sent and summed in bfloat16 or wider, within the bound.
No kernel may reach another device: no remote copies, remote signals or barrier semaphores. Data moves between devices by JAX's collectives and lax.ppermute only.
A program may use at most 64 MiB of HBM per device.

v0:
```python
import jax
import jax.numpy as jnp
from jax import lax
from jax.sharding import PartitionSpec as P

ADAPTER_COUNT = 512
CAP = 4


def pack_slots(row_adapter_index):
    labels = row_adapter_index[:, 0]
    position = jnp.arange(labels.shape[0], dtype=jnp.int32)
    matching = (labels[:, None] == labels[None, :]) & (position[:, None] > position[None, :])
    before = jnp.sum(matching.astype(jnp.int32), axis=1)
    return labels * CAP + before


def apply_adapter(tokens, cache_slot_index, adapter_down_weight, adapter_up_weight):
    owners = lax.axis_size("adapter")
    feature_width = tokens.shape[1]
    resident_adapters = adapter_down_weight.shape[0]
    column_span = adapter_up_weight.shape[2]
    outbox = (
        jnp.zeros((ADAPTER_COUNT * CAP, feature_width), jnp.bfloat16)
        .at[cache_slot_index]
        .set(tokens)
    )
    received_rows = lax.all_to_all(
        outbox.reshape(owners, resident_adapters * CAP, feature_width),
        "adapter",
        split_axis=0,
        concat_axis=0,
        tiled=True,
    )
    received_rows = received_rows.reshape(owners, resident_adapters, CAP, feature_width)
    partial_rank = jnp.einsum(
        "omjg,mgb->omjb", received_rows, adapter_down_weight, preferred_element_type=jnp.float32
    )
    summed_rank = lax.psum(partial_rank.astype(jnp.bfloat16), "tensor")
    update = jnp.einsum(
        "sacr,aro->saco", summed_rank, adapter_up_weight, preferred_element_type=jnp.float32
    ).astype(jnp.bfloat16)
    returned = lax.all_to_all(
        update.reshape(owners, resident_adapters * CAP, column_span),
        "adapter",
        split_axis=0,
        concat_axis=0,
        tiled=True,
    )
    return returned.reshape(ADAPTER_COUNT * CAP, column_span)[cache_slot_index]


def project(tokens, key_value_weight):
    partial_sum = jnp.dot(tokens, key_value_weight, preferred_element_type=jnp.float32)
    return lax.psum_scatter(
        partial_sum.astype(jnp.bfloat16), "tensor", scatter_dimension=1, tiled=True
    ).astype(jnp.float32)


def per_device(
    tokens,
    row_adapter_index,
    adapter_down_weight,
    adapter_up_weight,
    key_value_weight,
    accepted_branch_rows,
    owner_cache_slots,
):
    cache_slot_index = pack_slots(row_adapter_index)
    base = project(tokens, key_value_weight)
    update_row_block = apply_adapter(
        tokens, cache_slot_index, adapter_down_weight, adapter_up_weight
    )
    key_value = (base + update_row_block.astype(jnp.float32)).astype(jnp.bfloat16)
    owners = lax.axis_size("adapter")
    column_span = key_value.shape[1]
    chosen = key_value[accepted_branch_rows.reshape(-1)]
    moved = lax.all_to_all(
        chosen.reshape(owners, -1, column_span), "adapter", split_axis=0, concat_axis=0, tiled=True
    )
    targets = owner_cache_slots.reshape(-1)
    decode_cache = (
        jnp.zeros((targets.shape[0], column_span), jnp.bfloat16)
        .at[targets]
        .set(moved.reshape(-1, column_span))
    )
    return (key_value, decode_cache)


def solution(mesh):
    in_specs = (
        P("adapter", "tensor"),
        P("adapter", None),
        P("adapter", "tensor", None),
        P("adapter", None, "tensor"),
        P("tensor", None),
        P("adapter", None, None),
        P(None, "adapter", None),
    )
    out_specs = (P("adapter", "tensor"), P("adapter", "tensor"))
    return jax.shard_map(
        per_device, mesh=mesh, in_specs=in_specs, out_specs=out_specs, check_vma=False
    )
```

profile of v0, /device:TPU:2, one launch (start us, length us, event | category | flops | bytes accessed | tf_op | source)
XLA Modules:
  0.0 294.2 jit_solution(5736376576717085041)
XLA Ops:
  7.2 0.0 copy-start
  7.2 0.0 all-reduce.2.cloned.1.call-start
  7.2 1.4 convert_reduce_fusion
  8.6 0.7 compare_select_fusion
  9.3 7.2 %scatter_custom_fusion = bf16[2048,512]{1,0:T(8,128)(2,1)} fusion(s32[1024]{0:T(1024)S(1)} %bitcast.42, bf16[1024,512]{1,0:T(8,128)(2,1)} %param.7, bf16[]{:T(256)} %constant.6.clone.1), kind=kCustom, calls=%fused_computation.12 | custom fusion | bytes 2097664 | tf_op jit(solution)/shard_map/scatter | solution.py:26
  16.5 62.0 %all_to_all.15 = bf16[32,64,512]{2,1,0:T(8,128)(2,1)S(1)} all-to-all(bf16[32,64,512]{2,1,0:T(8,128)(2,1)} %bitcast.37), channel_id=1, replica_groups=mesh['adapter'=32,'tensor'=16] {'adapter'}, dimensions={0} | all-to-all | bytes 4194304 | tf_op jit(solution)/shard_map/all_to_all | solution.py:28
  78.5 1.2 copy.23
  79.6 0.1 copy-done.5
  79.7 1.5 fusion.1
  81.2 0.0 all-reduce.2.cloned.1.call-update
  81.2 0.0 reduce-scatter.4.cloned.1.call-start
  81.3 4.3 %convolution_convert_fusion = bf16[1024,2048]{1,0:T(8,128)(2,1)} fusion(bf16[1024,512]{1,0:T(8,128)(2,1)S(1)} %copy-done.6, bf16[512,2048]{1,0:T(8,128)(2,1)S(1)} %copy-done), kind=kOutput, calls=%fused_computation.7 | convolution fusion | flops 2149580800 | bytes 7340032 | tf_op jit(solution)/shard_map/dot_general | solution.py:54
  85.7 6.4 %copy.29 = bf16[1024,2048]{0,1:T(8,128)(2,1)} copy(bf16[1024,2048]{1,0:T(8,128)(2,1)} %convolution_convert_fusion) | data formatting | bytes 8388608
  92.1 0.0 reduce-scatter.4.cloned.1.call-update
  92.1 103.0 %all-reduce.2.cloned.1.call-done = bf16[32,16,4,64]{3,0,2,1:T(8,128)(2,1)} async-done(((bf16[32,16,4,64]{3,0,2,1:T(8,128)(2,1)}), bf16[32,16,4,64]{3,0,2,1:T(8,128)(2,1)}) %all-reduce.2.cloned.1.call-update) | async-done | bytes 262160 | tf_op jit(solution)/shard_map/psum | solution.py:39
  195.1 1.3 convolution_convert_fusion.1
  196.4 1.0 copy.24
  197.4 10.5 %all-to-all-start.1 = ((bf16[32,64,128]{2,1,0:T(8,128)(2,1)}), bf16[32,64,128]{2,1,0:T(8,128)(2,1)S(1)}, u32[]{:S(2)}, u32[]{:S(2)}) async-start(bf16[32,64,128]{2,1,0:T(8,128)(2,1)} %copy.24), calls=%async_computation.1 | async-start | bytes 1048576 | tf_op jit(solution)/shard_map/all_to_all | solution.py:43
  208.0 0.1 copy.26
  208.1 0.1 reshape.91
  208.2 0.1 copy.25
  208.3 0.1 reshape.90
  208.4 15.1 %all-to-all-done.1 = bf16[32,64,128]{2,1,0:T(8,128)(2,1)S(1)} async-done(((bf16[32,64,128]{2,1,0:T(8,128)(2,1)}), bf16[32,64,128]{2,1,0:T(8,128)(2,1)S(1)}, u32[]{:S(2)}, u32[]{:S(2)}) %all-to-all-start.1) | async-done | bytes 524320 | tf_op jit(solution)/shard_map/all_to_all | solution.py:43
  223.5 3.2 %gather_fusion = bf16[1024,128]{1,0:T(8,128)(2,1)S(1)} fusion(bf16[2048,128]{1,0:T(8,128)(2,1)S(1)} %bitcast.36, s32[1024]{0:T(1024)S(1)} %broadcast_clamp_fusion), kind=kCustom, calls=%fused_computation | custom fusion | bytes 528384 | tf_op jit(solution)/shard_map/gather | solution.py:50
  226.7 37.5 %reduce-scatter.4.cloned.1.call-done = bf16[128,1024]{1,0:T(8,128)(2,1)} async-done(((bf16[2048,1024]{1,0:T(8,128)(2,1)}), bf16[128,1024]{1,0:T(8,128)(2,1)}) %reduce-scatter.4.cloned.1.call-update) | async-done | bytes 262160
  264.1 1.1 copy.30
  265.3 0.1 add_convert_fusion
  265.4 0.0 copy-start.1
  265.4 1.3 gather_fusion.1
  266.7 10.5 %all-to-all-start.2 = ((bf16[32,4,128]{2,1,0:T(4,128)(2,1)}), bf16[32,4,128]{2,1,0:T(4,128)(2,1)S(1)}, u32[]{:S(2)}, u32[]{:S(2)}) async-start(bf16[32,4,128]{2,1,0:T(4,128)(2,1)} %bitcast.15), calls=%async_computation.2 | async-start | bytes 65536 | tf_op jit(solution)/shard_map/all_to_all | solution.py:78
  277.2 8.7 %all-to-all-done.2 = bf16[32,4,128]{2,1,0:T(4,128)(2,1)S(1)} async-done(((bf16[32,4,128]{2,1,0:T(4,128)(2,1)}), bf16[32,4,128]{2,1,0:T(4,128)(2,1)S(1)}, u32[]{:S(2)}, u32[]{:S(2)}) %all-to-all-start.2) | async-done | bytes 32800 | tf_op jit(solution)/shard_map/all_to_all | solution.py:78
  285.9 1.4 scatter_custom_fusion.1
  (15 shorter events, 0.0 us)
Async XLA Ops:
  7.2 74.1 %copy-start = (bf16[512,2048]{1,0:T(8,128)(2,1)S(1)}, bf16[512,2048]{1,0:T(8,128)(2,1)}, u32[]{:S(2)}) copy-start(bf16[512,2048]{1,0:T(8,128)(2,1)} %param.11) | copy-start | bytes 6291460
  7.2 187.9 %all-reduce.2.cloned.1.call-start = ((), (), s32[]{:S(2)}) async-start(), calls=%async_computation.4 | async-start | bytes 1048576 | tf_op jit(solution)/shard_map/psum | solution.py:39
  78.5 1.2 copy-start.5
  79.7 1.6 copy-start.6
  81.2 182.9 %reduce-scatter.4.cloned.1.call-start = ((), (), s32[]{:S(2)}) async-start(), calls=%async_computation.5 | async-start | bytes 4456448
  92.1 103.0 %copy-start.2 = (bf16[16,64,128]{2,1,0:T(8,128)(2,1)S(1)}, bf16[16,64,128]{2,1,0:T(8,128)(2,1)}, u32[]{:S(2)}) copy-start(bf16[16,64,128]{2,1,0:T(8,128)(2,1)} %param.10) | copy-start | bytes 786436
  92.1 115.9 %copy-start.3 = (s32[1,32,4]{1,2,0:T(4,128)S(1)}, s32[1,32,4]{1,2,0:T(4,128)}, u32[]{:S(2)}) copy-start(s32[1,32,4]{1,2,0:T(4,128)} %param.12) | copy-start | bytes 1540
  92.1 116.1 %copy-start.4 = (s32[32,1,4]{0,2,1:T(4,128)S(1)}, s32[32,1,4]{0,2,1:T(4,128)}, u32[]{:S(2)}) copy-start(s32[32,1,4]{0,2,1:T(4,128)} %param.13) | copy-start | bytes 1540
  197.4 26.1 %all-to-all-start.1 = ((bf16[32,64,128]{2,1,0:T(8,128)(2,1)}), bf16[32,64,128]{2,1,0:T(8,128)(2,1)S(1)}, u32[]{:S(2)}, u32[]{:S(2)}) async-start(bf16[32,64,128]{2,1,0:T(8,128)(2,1)} %copy.24), calls=%async_computation.1 | async-start | bytes 1048576 | tf_op jit(solution)/shard_map/all_to_all | solution.py:43
  265.4 22.0 %copy-start.1 = (bf16[1024,128]{1,0:T(8,128)(2,1)}, bf16[1024,128]{1,0:T(8,128)(2,1)S(1)}, u32[]{:S(2)}) copy-start(bf16[1024,128]{1,0:T(8,128)(2,1)S(1)} %add_convert_fusion) | copy-start | bytes 786436
  266.7 19.2 %all-to-all-start.2 = ((bf16[32,4,128]{2,1,0:T(4,128)(2,1)}), bf16[32,4,128]{2,1,0:T(4,128)(2,1)S(1)}, u32[]{:S(2)}, u32[]{:S(2)}) async-start(bf16[32,4,128]{2,1,0:T(4,128)(2,1)} %bitcast.15), calls=%async_computation.2 | async-start | bytes 65536 | tf_op jit(solution)/shard_map/all_to_all | solution.py:78
Sparse Core Ops, SparseCore 0:
  81.4 113.6 all-reduce.1
  198.1 65.9 reduce-scatter.3
where the time goes:
time: 295 us; the launch traced here: 294 us
  waiting for transfers between devices  164 us (56%)
  blocking collectives  62 us (21%)
  local copies, waits for them, and re-layouts  23.3 us (8%)
  starting transfers between devices  21.1 us (7%)
  between operations  14.2 us (5%)
  matrix products  7.18 us (2%)
    psum x1, waiting for transfers between devices, apply_adapter(): summed_rank = lax.psum(partial_rank.astype(jnp.bfloat16), 'tensor')  103 us
    all_to_all x1, blocking collectives, apply_adapter(): lax.all_to_all(outbox.reshape(owners, resident_adapters * CAP, feature_wi...  62 us
    unnamed x3, waiting for transfers between devices  37.5 us
    all_to_all x1, waiting for transfers between devices, apply_adapter(): lax.all_to_all(update.reshape(owners, resident_adapters * CAP, column_spa...  15.1 us
    all_to_all x1, starting transfers between devices, apply_adapter(): lax.all_to_all(update.reshape(owners, resident_adapters * CAP, column_spa...  10.5 us
    all_to_all x1, starting transfers between devices, per_device(): lax.all_to_all(chosen.reshape(owners, -1, column_span), 'adapter', split_...  10.5 us
    all_to_all x1, waiting for transfers between devices, per_device(): lax.all_to_all(chosen.reshape(owners, -1, column_span), 'adapter', split_...  8.66 us
    unnamed x18, local copies, waits for them, and re-layouts  7.78 us
  transfers between devices with their start and end apart: 4, of which 4 were waited for; matrix products, arithmetic and copies ran while one was open for 6% of the time, Pallas kernels for 0%

commit v1 on v0

--- a/solution.py
+++ b/solution.py
@@ -36,7 +36,7 @@
     partial_rank = jnp.einsum(
         "omjg,mgb->omjb", received_rows, adapter_down_weight, preferred_element_type=jnp.float32
     )
-    summed_rank = lax.psum(partial_rank.astype(jnp.bfloat16), "tensor")
+    summed_rank = jnp.sum(lax.all_gather(partial_rank.astype(jnp.bfloat16), "tensor"), axis=0)
     update = jnp.einsum(
         "sacr,aro->saco", summed_rank, adapter_up_weight, preferred_element_type=jnp.float32
     ).astype(jnp.bfloat16)

time: 295 us -> 239 us (0.81)
  waiting for transfers between devices: 164 us -> 105 us
  other arithmetic: 2.16 us -> 7.65 us
    psum x1 -> x0, waiting for transfers between devices: 103 us -> none  [apply_adapter(): summed_rank = lax.psum(partial_rank.astype(jnp.bfloat16), 'tensor')]
    all_gather x0 -> x1, waiting for transfers between devices: none -> 46.4 us  [apply_adapter(): lax.all_gather(partial_rank.astype(jnp.bfloat16), 'tensor')]
    all_to_all x1, waiting for transfers between devices: 15.1 us -> 0.01 us  [apply_adapter(): lax.all_to_all(update.reshape(owners, resident_adapters * CAP, column_spa...]
    unnamed x3, waiting for transfers between devices: 37.5 us -> 49.5 us
    reduce_sum x0 -> x1, other arithmetic: none -> 5.5 us  [apply_adapter(): jnp.sum(lax.all_gather(partial_rank.astype(jnp.bfloat16), 'tensor'), axis=0)]
  transfers between devices with their start and end apart: 4 -> 4, of which waited for: 4 -> 3; matrix products, arithmetic and copies ran while one was open for 6% -> 8% of each run, Pallas kernels for 0% -> 0%
where the time goes in v1:
time: 239 us
  waiting for transfers between devices  105 us (44%)
  blocking collectives  62 us (26%)
  local copies, waits for them, and re-layouts  23.3 us (10%)
  starting transfers between devices  20.9 us (9%)
  between operations  14.2 us (6%)
  other arithmetic  7.65 us (3%)
  matrix products  6.07 us (3%)
    all_to_all x1, blocking collectives, apply_adapter(): lax.all_to_all(outbox.reshape(owners, resident_adapters * CAP, feature_wi...  62 us
    unnamed x3, waiting for transfers between devices  49.5 us
    all_gather x1, waiting for transfers between devices, apply_adapter(): lax.all_gather(partial_rank.astype(jnp.bfloat16), 'tensor')  46.4 us
    all_to_all x1, starting transfers between devices, apply_adapter(): lax.all_to_all(update.reshape(owners, resident_adapters * CAP, column_spa...  10.5 us
    all_to_all x1, starting transfers between devices, per_device(): lax.all_to_all(chosen.reshape(owners, -1, column_span), 'adapter', split_...  10.3 us
    all_to_all x1, waiting for transfers between devices, per_device(): lax.all_to_all(chosen.reshape(owners, -1, column_span), 'adapter', split_...  8.66 us
    unnamed x18, local copies, waits for them, and re-layouts  7.78 us
    scatter x1, local copies, waits for them, and re-layouts, apply_adapter(): outbox = jnp.zeros((ADAPTER_COUNT * CAP, feature_width), jnp.bfloat16).at...  7.17 us
  transfers between devices with their start and end apart: 4, of which 3 were waited for; matrix products, arithmetic and copies ran while one was open for 8% of the time, Pallas kernels for 0%

profile of v1, /device:TPU:2, one launch (start us, length us, event | category | flops | bytes accessed | tf_op | source)
XLA Modules:
  0.0 238.7 jit_solution(15358108926720213912)
XLA Ops:
  7.2 0.0 copy-start
  7.2 0.0 all-gather.3.cloned.1.call-start
  7.2 1.4 convert_reduce_fusion
  8.6 0.7 compare_select_fusion
  9.3 7.2 %scatter_custom_fusion = bf16[2048,512]{1,0:T(8,128)(2,1)} fusion(s32[1024]{0:T(1024)S(1)} %bitcast.44, bf16[1024,512]{1,0:T(8,128)(2,1)} %param.7, bf16[]{:T(256)} %constant.6.clone.1), kind=kCustom, calls=%fused_computation.12 | custom fusion | bytes 2097664 | tf_op jit(solution)/shard_map/scatter | solution.py:26
  16.5 62.0 %all_to_all.15 = bf16[32,64,512]{2,1,0:T(8,128)(2,1)S(1)} all-to-all(bf16[32,64,512]{2,1,0:T(8,128)(2,1)} %bitcast.39), channel_id=1, replica_groups=mesh['adapter'=32,'tensor'=16] {'adapter'}, dimensions={0} | all-to-all | bytes 4194304 | tf_op jit(solution)/shard_map/all_to_all | solution.py:28
  78.5 1.2 copy.20
  79.6 0.1 copy-done.5
  79.7 1.5 fusion.1
  81.2 0.0 all-gather.3.cloned.1.call-update
  81.2 0.0 reduce-scatter.4.cloned.1.call-start
  81.3 4.3 %convolution_convert_fusion = bf16[1024,2048]{1,0:T(8,128)(2,1)} fusion(bf16[1024,512]{1,0:T(8,128)(2,1)S(1)} %copy-done.6, bf16[512,2048]{1,0:T(8,128)(2,1)S(1)} %copy-done), kind=kOutput, calls=%fused_computation.7 | convolution fusion | flops 2149580800 | bytes 7340032 | tf_op jit(solution)/shard_map/dot_general | solution.py:54
  85.6 6.4 %copy.26 = bf16[1024,2048]{0,1:T(8,128)(2,1)} copy(bf16[1024,2048]{1,0:T(8,128)(2,1)} %convolution_convert_fusion) | data formatting | bytes 8388608
  92.0 0.0 reduce-scatter.4.cloned.1.call-update
  92.0 46.4 %all-gather.3.cloned.1.call-done = bf16[512,16,4,64]{3,0,2,1:T(8,128)(2,1)} async-done(((bf16[32,16,4,64]{3,0,2,1:T(8,128)(2,1)}), bf16[512,16,4,64]{3,0,2,1:T(8,128)(2,1)}) %all-gather.3.cloned.1.call-update) | async-done | bytes 4194320 | tf_op jit(solution)/shard_map/all_gather | solution.py:39
  138.4 5.5 %reduce_sum.25 = bf16[32,16,4,64]{3,0,2,1:T(8,128)(2,1)S(1)} reduce(bf16[16,32,16,4,64]{4,1,0,3,2:T(8,128)(2,1)} %bitcast.38, bf16[]{:T(256)} %constant.6.clone.1), dimensions={0}, to_apply=%region_3.0 | reduce | flops 1966080 | bytes 4456450 | tf_op jit(solution)/shard_map/reduce_sum | solution.py:39
  143.9 0.3 convolution_convert_fusion.1
  144.2 1.0 copy.21
  145.2 10.5 %all-to-all-start.1 = ((bf16[32,64,128]{2,1,0:T(8,128)(2,1)}), bf16[32,64,128]{2,1,0:T(8,128)(2,1)S(1)}, u32[]{:S(2)}, u32[]{:S(2)}) async-start(bf16[32,64,128]{2,1,0:T(8,128)(2,1)} %copy.21), calls=%async_computation.1 | async-start | bytes 1048576 | tf_op jit(solution)/shard_map/all_to_all | solution.py:43
  155.7 0.1 copy.23
  155.8 0.1 reshape.91
  155.9 0.1 copy.22
  156.0 0.1 reshape.90
  156.2 49.4 %reduce-scatter.4.cloned.1.call-done = bf16[128,1024]{1,0:T(8,128)(2,1)} async-done(((bf16[2048,1024]{1,0:T(8,128)(2,1)}), bf16[128,1024]{1,0:T(8,128)(2,1)}) %reduce-scatter.4.cloned.1.call-update) | async-done | bytes 262160
  205.6 1.1 copy.27
  206.8 3.2 %gather_fusion = bf16[1024,128]{1,0:T(8,128)(2,1)S(1)} fusion(bf16[2048,128]{1,0:T(8,128)(2,1)S(1)} %bitcast.37, s32[1024]{0:T(1024)S(1)} %broadcast_clamp_fusion), kind=kCustom, calls=%fused_computation | custom fusion | bytes 528384 | tf_op jit(solution)/shard_map/gather | solution.py:50
  210.0 0.1 add_convert_fusion
  210.1 0.0 copy-start.1
  210.1 1.3 gather_fusion.1
  211.4 10.3 %all-to-all-start.2 = ((bf16[32,4,128]{2,1,0:T(4,128)(2,1)}), bf16[32,4,128]{2,1,0:T(4,128)(2,1)S(1)}, u32[]{:S(2)}, u32[]{:S(2)}) async-start(bf16[32,4,128]{2,1,0:T(4,128)(2,1)} %bitcast.16), calls=%async_computation.2 | async-start | bytes 65536 | tf_op jit(solution)/shard_map/all_to_all | solution.py:78
  221.7 8.7 %all-to-all-done.2 = bf16[32,4,128]{2,1,0:T(4,128)(2,1)S(1)} async-done(((bf16[32,4,128]{2,1,0:T(4,128)(2,1)}), bf16[32,4,128]{2,1,0:T(4,128)(2,1)S(1)}, u32[]{:S(2)}, u32[]{:S(2)}) %all-to-all-start.2) | async-done | bytes 32800 | tf_op jit(solution)/shard_map/all_to_all | solution.py:78
  230.4 1.4 scatter_custom_fusion.1
  (16 shorter events, 0.0 us)
Async XLA Ops:
  7.2 74.1 %copy-start = (bf16[512,2048]{1,0:T(8,128)(2,1)S(1)}, bf16[512,2048]{1,0:T(8,128)(2,1)}, u32[]{:S(2)}) copy-start(bf16[512,2048]{1,0:T(8,128)(2,1)} %param.11) | copy-start | bytes 6291460
  7.2 131.2 %all-gather.3.cloned.1.call-start = ((), (), s32[]{:S(2)}) async-start(), calls=%async_computation.4 | async-start | bytes 8912896 | tf_op jit(solution)/shard_map/all_gather | solution.py:39
  78.5 1.2 copy-start.5
  79.7 1.6 copy-start.6
  81.2 124.4 %reduce-scatter.4.cloned.1.call-start = ((), (), s32[]{:S(2)}) async-start(), calls=%async_computation.5 | async-start | bytes 4456448
  138.4 5.5 %copy-start.2 = (bf16[16,64,128]{2,1,0:T(8,128)(2,1)S(1)}, bf16[16,64,128]{2,1,0:T(8,128)(2,1)}, u32[]{:S(2)}) copy-start(bf16[16,64,128]{2,1,0:T(8,128)(2,1)} %param.10) | copy-start | bytes 786436
  143.9 11.8 %copy-start.3 = (s32[1,32,4]{1,2,0:T(4,128)S(1)}, s32[1,32,4]{1,2,0:T(4,128)}, u32[]{:S(2)}) copy-start(s32[1,32,4]{1,2,0:T(4,128)} %param.12) | copy-start | bytes 1540
  143.9 12.0 %copy-start.4 = (s32[32,1,4]{0,2,1:T(4,128)S(1)}, s32[32,1,4]{0,2,1:T(4,128)}, u32[]{:S(2)}) copy-start(s32[32,1,4]{0,2,1:T(4,128)} %param.13) | copy-start | bytes 1540
  145.2 61.5 %all-to-all-start.1 = ((bf16[32,64,128]{2,1,0:T(8,128)(2,1)}), bf16[32,64,128]{2,1,0:T(8,128)(2,1)S(1)}, u32[]{:S(2)}, u32[]{:S(2)}) async-start(bf16[32,64,128]{2,1,0:T(8,128)(2,1)} %copy.21), calls=%async_computation.1 | async-start | bytes 1048576 | tf_op jit(solution)/shard_map/all_to_all | solution.py:43
  210.1 21.8 %copy-start.1 = (bf16[1024,128]{1,0:T(8,128)(2,1)}, bf16[1024,128]{1,0:T(8,128)(2,1)S(1)}, u32[]{:S(2)}) copy-start(bf16[1024,128]{1,0:T(8,128)(2,1)S(1)} %add_convert_fusion) | copy-start | bytes 786436
  211.4 19.0 %all-to-all-start.2 = ((bf16[32,4,128]{2,1,0:T(4,128)(2,1)}), bf16[32,4,128]{2,1,0:T(4,128)(2,1)S(1)}, u32[]{:S(2)}, u32[]{:S(2)}) async-start(bf16[32,4,128]{2,1,0:T(4,128)(2,1)} %bitcast.16), calls=%async_computation.2 | async-start | bytes 65536 | tf_op jit(solution)/shard_map/all_to_all | solution.py:78
Sparse Core Ops, SparseCore 0:
  81.3 57.0 all-gather.2
  141.2 64.3 reduce-scatter.3
